TPU v7x, 32 devices: a whole 2x2x4 slice. The times are simulated.
32 devices in a mesh: dp: 8 (over z, x), seq: 4 (over y, core).
Axes of the slice: x: 2, y: 2, z: 4, core: 2. Of those that a mesh axis runs over, the one named last changes fastest.
Arguments:
- inputs: bfloat16 [8, 1024, 768], P('dp', 'seq'), may hold values from -6 to 6
- cotangent: bfloat16 [8, 1024, 768], P('dp', 'seq'), may hold values from -6 to 6
- image_lengths: int32 [8, 8], P('dp'), may hold values from 1 to 384, 1024 in all within a row
- attention_weight: float32 [2, 4, 768, 768], P(None, None, ('dp', 'seq')), may hold values from -1.299038 to 1.299038
- attention_moment: float32 [2, 4, 768, 768], P(None, None, ('dp', 'seq')), may hold values from -56 to 56
- attention_average: float32 [2, 4, 768, 768], P(None, None, ('dp', 'seq')), may hold values from -0.21875 to 0.21875
- up_weight: float32 [2, 768, 3072], P(None, ('dp', 'seq')), may hold values from -0.21875 to 0.21875
- up_moment: float32 [2, 768, 3072], P(None, ('dp', 'seq')), may hold values from -112 to 112
- up_average: float32 [2, 768, 3072], P(None, ('dp', 'seq')), may hold values from -0.21875 to 0.21875
- down_weight: float32 [2, 3072, 768], P(None, ('dp', 'seq')), may hold values from -0.109375 to 0.109375
- down_moment: float32 [2, 3072, 768], P(None, ('dp', 'seq')), may hold values from -256 to 256
- down_average: float32 [2, 3072, 768], P(None, ('dp', 'seq')), may hold values from -0.109375 to 0.109375
- layer_vectors: float32 [2, 8, 768], P(None, None, ('dp', 'seq')), may hold values from -0.6 to 1.6
- vector_moment: float32 [2, 8, 768], P(None, None, ('dp', 'seq')), may hold values from -256 to 256
- vector_average: float32 [2, 8, 768], P(None, None, ('dp', 'seq')), may hold values from -0.6 to 1.6
- hidden_bias: float32 [2, 3072], P(None, ('dp', 'seq')), may hold values from -1.5 to 1.5
- bias_moment: float32 [2, 3072], P(None, ('dp', 'seq')), may hold values from -112 to 112
- bias_average: float32 [2, 3072], P(None, ('dp', 'seq')), may hold values from -1.5 to 1.5
Outputs:
- output: bfloat16 [8, 1024, 768], P('dp', 'seq')
- input_grad: bfloat16 [8, 1024, 768], P('dp', 'seq')
- attention_grad: float32 [2, 4, 768, 768], P(None, None, ('dp', 'seq'))
- attention_moment_new: float32 [2, 4, 768, 768], P(None, None, ('dp', 'seq'))
- attention_average_new: float32 [2, 4, 768, 768], P(None, None, ('dp', 'seq'))
- attention_weight_new: float32 [2, 4, 768, 768], P(None, None, ('dp', 'seq'))
- attention_weight_copy: bfloat16 [2, 4, 768, 768], P(None, None, ('dp', 'seq'))
- up_grad: float32 [2, 768, 3072], P(None, ('dp', 'seq'))
- up_moment_new: float32 [2, 768, 3072], P(None, ('dp', 'seq'))
- up_average_new: float32 [2, 768, 3072], P(None, ('dp', 'seq'))
- up_weight_new: float32 [2, 768, 3072], P(None, ('dp', 'seq'))
- up_weight_copy: bfloat16 [2, 768, 3072], P(None, ('dp', 'seq'))
- down_grad: float32 [2, 3072, 768], P(None, ('dp', 'seq'))
- down_moment_new: float32 [2, 3072, 768], P(None, ('dp', 'seq'))
- down_average_new: float32 [2, 3072, 768], P(None, ('dp', 'seq'))
- down_weight_new: float32 [2, 3072, 768], P(None, ('dp', 'seq'))
- down_weight_copy: bfloat16 [2, 3072, 768], P(None, ('dp', 'seq'))
- vector_grad: float32 [2, 8, 768], P(None, None, ('dp', 'seq'))
- vector_moment_new: float32 [2, 8, 768], P(None, None, ('dp', 'seq'))
- vector_average_new: float32 [2, 8, 768], P(None, None, ('dp', 'seq'))
- layer_vectors_new: float32 [2, 8, 768], P(None, None, ('dp', 'seq'))
- layer_vectors_copy: bfloat16 [2, 8, 768], P(None, None, ('dp', 'seq'))
- bias_grad: float32 [2, 3072], P(None, ('dp', 'seq'))
- bias_moment_new: float32 [2, 3072], P(None, ('dp', 'seq'))
- bias_average_new: float32 [2, 3072], P(None, ('dp', 'seq'))
- hidden_bias_new: float32 [2, 3072], P(None, ('dp', 'seq'))
- hidden_bias_copy: bfloat16 [2, 3072], P(None, ('dp', 'seq'))
Inputs may be any that keep to these rules, and one draw needn't show every extreme that they name: `image_lengths`: in each row the first 7 entries are image lengths and the last is the padding; a row's entries sum to 1024, and its largest entry is 384.
All inputs are finite; a program needn't handle non-finite values.
Results may differ from a plain program's by a relative error of at most 0.014.
Values may be sent and summed in bfloat16 or wider, within the bound.
A program may use at most 320 MiB of HBM per device.

v0:
```python
import functools
import math

import jax
import jax.numpy as jnp
from jax import lax
from jax.experimental import pallas as pl
from jax.experimental.pallas import tpu as pltpu
from jax.sharding import PartitionSpec as P

HEAD_DIM = 64
SEGS = 8


EPSILON = 1e-06
SCALE_SCORE = 0.125
MOMENTUM_RATE = 0.9
DECAY_RATE = 0.0001
AVERAGE_RATE = 0.5
LEARN_BASE = 0.1
VMEM_BYTES = 66900000


def as_sent(shard):
    return jax.tree.map(lambda a: a.astype(jnp.bfloat16) if a.dtype == jnp.float32 else a, shard)


def layer_norm(values, gain_row, shift_row):
    center = values - jnp.mean(values, axis=-1, keepdims=True)
    spread = jnp.mean(center * center, axis=-1, keepdims=True)
    return center * lax.rsqrt(spread + EPSILON) * gain_row + shift_row


def gelu_exact(values):
    return jax.nn.gelu(values, approximate=False)


def project(values, matrix):
    return jnp.einsum("rti,ij->rtj", values, matrix, preferred_element_type=jnp.float32)


def project_back(grad_rows, matrix):
    return jnp.einsum("rtj,ij->rti", grad_rows, matrix, preferred_element_type=jnp.float32)


def outer_sum(values, grad_rows):
    return jnp.einsum("rti,rtj->ij", values, grad_rows, preferred_element_type=jnp.float32)


def column_sum(grad_rows):
    return jnp.sum(grad_rows, axis=(0, 1), dtype=jnp.float32)


def segment_ids(image_lengths, row_len):
    upto = jnp.arange(SEGS)[:, None] <= jnp.arange(SEGS)[None, :]
    bounds = jnp.sum(jnp.where(upto[None], image_lengths[:, :, None], 0), axis=1, dtype=jnp.int32)
    places = jnp.arange(row_len, dtype=jnp.int32)
    return jnp.sum(
        (bounds[:, None, :] <= places[None, :, None]).astype(jnp.int32), axis=-1, dtype=jnp.int32
    )


def visible_block(seg_rows, offset, block_size):
    row_len = seg_rows.shape[0]
    seg_query = seg_rows[offset : offset + block_size]
    matching = seg_query[:, None] == seg_rows[None, :]
    open_key = seg_rows[None, :] != SEGS - 1
    query_place = offset + jnp.arange(block_size, dtype=jnp.int32)
    key_place = jnp.arange(row_len, dtype=jnp.int32)
    return matching & open_key | (query_place[:, None] == key_place[None, :])


def score_block(query_block, key_heads, seg_rows, offset):
    scores = (
        jnp.einsum("qhd,khd->hqk", query_block, key_heads, preferred_element_type=jnp.float32)
        * SCALE_SCORE
    )
    allowed = visible_block(seg_rows, offset, query_block.shape[0])
    return jnp.where(allowed[None], scores, -1e30)


def split_heads(row_values):
    return row_values.reshape(row_values.shape[0], row_values.shape[1] // HEAD_DIM, HEAD_DIM)


def attend_row(row_items):
    query_row, key_row, value_row, seg_rows = row_items
    row_len = query_row.shape[0]
    query_heads = split_heads(query_row)
    key_heads = split_heads(key_row)
    value_heads = split_heads(value_row)
    block_size = min(512, row_len)
    outputs = []
    totals = []
    for offset in range(0, row_len, block_size):
        scores = score_block(query_heads[offset : offset + block_size], key_heads, seg_rows, offset)
        top_score = jnp.max(scores, axis=-1, keepdims=True)
        exponent = jnp.exp(scores - top_score)
        denominator = jnp.sum(exponent, axis=-1, keepdims=True)
        probability = (exponent / denominator).astype(jnp.bfloat16)
        outputs.append(
            jnp.einsum("hqk,khd->qhd", probability, value_heads, preferred_element_type=jnp.float32)
        )
        totals.append(top_score[..., 0] + jnp.log(denominator[..., 0]))
    mixture = jnp.concatenate(outputs, axis=0).reshape(query_row.shape).astype(jnp.bfloat16)
    return (mixture, jnp.concatenate(totals, axis=1))


def attend_back(row_items):
    query_row, key_row, value_row, grad_row, log_total, seg_rows = row_items
    row_len = query_row.shape[0]
    query_heads = split_heads(query_row)
    key_heads = split_heads(key_row)
    value_heads = split_heads(value_row)
    grad_heads = split_heads(grad_row)
    block_size = min(512, row_len)
    key_grad = jnp.zeros(key_heads.shape, jnp.float32)
    value_grad = jnp.zeros(value_heads.shape, jnp.float32)
    query_grads = []
    for offset in range(0, row_len, block_size):
        query_block = query_heads[offset : offset + block_size]
        grad_block = grad_heads[offset : offset + block_size]
        scores = score_block(query_block, key_heads, seg_rows, offset)
        probability = jnp.exp(scores - log_total[:, offset : offset + block_size, None])
        prob_low = probability.astype(jnp.bfloat16)
        prob_grad = jnp.einsum(
            "qhd,khd->hqk", grad_block, value_heads, preferred_element_type=jnp.float32
        )
        inner_sum = jnp.sum(probability * prob_grad, axis=-1, keepdims=True)
        score_grad = (probability * (prob_grad - inner_sum)).astype(jnp.bfloat16)
        query_grads.append(
            jnp.einsum("hqk,khd->qhd", score_grad, key_heads, preferred_element_type=jnp.float32)
            * SCALE_SCORE
        )
        key_grad = (
            key_grad
            + jnp.einsum(
                "hqk,qhd->khd", score_grad, query_block, preferred_element_type=jnp.float32
            )
            * SCALE_SCORE
        )
        value_grad = value_grad + jnp.einsum(
            "hqk,qhd->khd", prob_low, grad_block, preferred_element_type=jnp.float32
        )
    flat_shape = query_row.shape
    query_grad = jnp.concatenate(query_grads, axis=0)
    return (
        query_grad.reshape(flat_shape).astype(jnp.bfloat16),
        key_grad.reshape(flat_shape).astype(jnp.bfloat16),
        value_grad.reshape(flat_shape).astype(jnp.bfloat16),
    )


def layer_forward(hidden_in, params, seg_full):
    attention, upward, downward, vectors, bias_up = params
    vector_values = vectors.astype(jnp.float32)
    normed = layer_norm(hidden_in, vector_values[0], vector_values[1]).astype(jnp.bfloat16)
    queries = (project(normed, attention[0]) + vector_values[2]).astype(jnp.bfloat16)
    key_rows = project(normed, attention[1]).astype(jnp.bfloat16)
    value_rows = (project(normed, attention[2]) + vector_values[3]).astype(jnp.bfloat16)
    query_full, key_full, value_full = (
        lax.all_to_all(queries, "seq", split_axis=2, concat_axis=1, tiled=True),
        lax.all_to_all(key_rows, "seq", split_axis=2, concat_axis=1, tiled=True),
        lax.all_to_all(value_rows, "seq", split_axis=2, concat_axis=1, tiled=True),
    )
    mixture, log_total = lax.map(attend_row, (query_full, key_full, value_full, seg_full))
    mixed_tokens = lax.all_to_all(mixture, "seq", split_axis=1, concat_axis=2, tiled=True)
    residual = hidden_in + (project(mixed_tokens, attention[3]) + vector_values[4])
    normed_two = layer_norm(residual, vector_values[5], vector_values[6]).astype(jnp.bfloat16)
    hidden_pre = project(normed_two, upward) + bias_up.astype(jnp.float32)
    hidden_act = gelu_exact(hidden_pre).astype(jnp.bfloat16)
    result = residual + (project(hidden_act, downward) + vector_values[7])
    saved_values = (
        hidden_in,
        normed,
        query_full,
        key_full,
        value_full,
        log_total,
        mixed_tokens,
        residual,
        normed_two,
        hidden_pre,
        hidden_act,
    )
    return (result, saved_values)


def layer_backward(grad_out, params, saved_values, seg_full):
    attention, upward, downward, vectors, bias_up = params
    vector_values = vectors.astype(jnp.float32)
    (
        hidden_in,
        normed,
        query_full,
        key_full,
        value_full,
        log_total,
        mixed_tokens,
        residual,
        normed_two,
        hidden_pre,
        hidden_act,
    ) = saved_values
    grad_mlp = grad_out.astype(jnp.bfloat16)
    grad_down = outer_sum(hidden_act, grad_mlp)
    grad_act = project_back(grad_mlp, downward)
    grad_pre = jax.vjp(gelu_exact, hidden_pre)[1](grad_act)[0].astype(jnp.bfloat16)
    grad_up = outer_sum(normed_two, grad_pre)
    grad_normed_two = project_back(grad_pre, upward)
    norm_pull_two = jax.vjp(layer_norm, residual, vector_values[5], vector_values[6])[1]
    grad_resid_norm, grad_gain_two, grad_shift_two = norm_pull_two(grad_normed_two)
    grad_residual = grad_out + grad_resid_norm
    grad_proj = grad_residual.astype(jnp.bfloat16)
    grad_outproj = outer_sum(mixed_tokens, grad_proj)
    grad_mixed = project_back(grad_proj, attention[3]).astype(jnp.bfloat16)
    grad_heads = lax.all_to_all(grad_mixed, "seq", split_axis=2, concat_axis=1, tiled=True)
    query_grad, key_grad, value_grad = lax.map(
        attend_back, (query_full, key_full, value_full, grad_heads, log_total, seg_full)
    )
    grad_query, grad_key, grad_value = (
        lax.all_to_all(query_grad, "seq", split_axis=1, concat_axis=2, tiled=True),
        lax.all_to_all(key_grad, "seq", split_axis=1, concat_axis=2, tiled=True),
        lax.all_to_all(value_grad, "seq", split_axis=1, concat_axis=2, tiled=True),
    )
    grad_wq = outer_sum(normed, grad_query)
    grad_wk = outer_sum(normed, grad_key)
    grad_wv = outer_sum(normed, grad_value)
    grad_normed = (
        project_back(grad_query, attention[0])
        + project_back(grad_key, attention[1])
        + project_back(grad_value, attention[2])
    )
    norm_pull_one = jax.vjp(layer_norm, hidden_in, vector_values[0], vector_values[1])[1]
    grad_in_norm, grad_gain_one, grad_shift_one = norm_pull_one(grad_normed)
    grad_in = grad_residual + grad_in_norm
    attention_terms = jnp.stack([grad_wq, grad_wk, grad_wv, grad_outproj])
    vector_terms = jnp.stack(
        [
            grad_gain_one,
            grad_shift_one,
            column_sum(grad_query),
            column_sum(grad_value),
            column_sum(grad_proj),
            grad_gain_two,
            grad_shift_two,
            column_sum(grad_mlp),
        ]
    )
    return (grad_in, (attention_terms, grad_up, grad_down, vector_terms, column_sum(grad_pre)))


def fold_terms(terms, dims, dp_count, seq_count):
    folded = []
    for member in range(len(terms)):
        term = terms[member]
        place = dims[member]
        shape = term.shape
        leading = math.prod(shape[:place])
        owned = shape[place] // (dp_count * seq_count)
        trailing = owned * math.prod(shape[place + 1 :])
        folded.append(term.reshape(leading, dp_count, seq_count, trailing))
    return tuple(folded)


def unfold_terms(received, terms, dims, dp_count, seq_count):
    results = []
    for member in range(len(terms)):
        shape = terms[member].shape
        place = dims[member]
        owned_shape = shape[:place] + (shape[place] // (dp_count * seq_count),) + shape[place + 1 :]
        results.append(jnp.sum(received[member], axis=(1, 2)).reshape(owned_shape))
    return tuple(results)


def optimizer_step(gradient, master, moment, average, step_rate):
    direction = gradient + DECAY_RATE * master
    moment_new = MOMENTUM_RATE * moment + direction
    master_new = master - step_rate * (direction + MOMENTUM_RATE * moment_new)
    average_new = AVERAGE_RATE * average + (1.0 - AVERAGE_RATE) * master_new
    return (gradient, moment_new, average_new, master_new, master_new.astype(jnp.bfloat16))


def plain_step(inputs, cotangent, image_lengths, masters):
    layer_count = masters[0].shape[0]
    dp_count = lax.axis_size("dp")
    seq_count = lax.axis_size("seq")
    seg_full = segment_ids(image_lengths, inputs.shape[1] * seq_count)

    def gather_layer(level_index):
        pieces = tuple((master[level_index].astype(jnp.bfloat16) for master in masters))
        return (
            lax.all_gather(pieces[0], ("dp", "seq"), axis=1, tiled=True),
            lax.all_gather(pieces[1], ("dp", "seq"), axis=0, tiled=True),
            lax.all_gather(pieces[2], ("dp", "seq"), axis=0, tiled=True),
            lax.all_gather(pieces[3], ("dp", "seq"), axis=1, tiled=True),
            lax.all_gather(pieces[4], ("dp", "seq"), axis=0, tiled=True),
        )

    hidden = inputs.astype(jnp.float32)
    kept_params = []
    kept_saved = []
    for level_index in range(layer_count):
        params = gather_layer(level_index)
        hidden, saved_values = layer_forward(hidden, params, seg_full)
        kept_params.append(params)
        kept_saved.append(saved_values)
    output = hidden.astype(jnp.bfloat16)
    stack_dims = (2, 1, 1, 2, 1)
    grad_hidden = cotangent.astype(jnp.float32)
    layer_terms = [None] * layer_count
    for level_index in reversed(range(layer_count)):
        params = kept_params[level_index]
        grad_hidden, terms_here = layer_backward(
            grad_hidden, params, kept_saved[level_index], seg_full
        )
        layer_terms[level_index] = terms_here
    stacked = tuple(
        (jnp.stack([terms_here[member] for terms_here in layer_terms]) for member in range(5))
    )
    folded = fold_terms(stacked, stack_dims, dp_count, seq_count)
    received = jax.tree.map(
        lambda part, own: part.astype(own.dtype),
        lax.all_to_all(
            lax.all_to_all(as_sent(folded), "dp", split_axis=1, concat_axis=1, tiled=True),
            "seq",
            split_axis=2,
            concat_axis=2,
            tiled=True,
        ),
        folded,
    )
    reduced = unfold_terms(received, stacked, stack_dims, dp_count, seq_count)
    return (output, grad_hidden.astype(jnp.bfloat16), *reduced)


MESH = pl.DeviceIdType.MESH
F32 = jnp.float32
BF16 = jnp.bfloat16
KEYS = 896
EDGE_KEYS = 640
QBLOCK = 256


def nt(left, right):
    return lax.dot_general(left, right, (((1,), (1,)), ((), ())), preferred_element_type=F32)


def nn(left, right):
    return lax.dot_general(left, right, (((1,), (0,)), ((), ())), preferred_element_type=F32)


def tn(left, right):
    return lax.dot_general(left, right, (((0,), (0,)), ((), ())), preferred_element_type=F32)


def norm_parts(values):
    center = values - jnp.mean(values, axis=-1, keepdims=True)
    scale = lax.rsqrt(jnp.mean(center * center, axis=-1, keepdims=True) + EPSILON)
    return center * scale, scale


def norm_back(values, grad, gain):
    unit, scale = norm_parts(values)
    pulled = grad * gain
    first = jnp.mean(pulled, axis=-1, keepdims=True)
    second = jnp.mean(pulled * unit, axis=-1, keepdims=True)
    result = scale * (pulled - first - unit * second)
    return (
        result,
        jnp.sum(grad * unit, axis=0, keepdims=True),
        jnp.sum(grad, axis=0, keepdims=True),
    )


SEMS = 178


def step_kernel(NZ, x_hbm, cot_hbm, lens, aw_hbm, uw_hbm, dw_hbm, lv, hb, *rest):
    (out, gin, gA_hbm, gU_hbm, gD_hbm, gV, gB) = rest[:7]
    (
        w1, w2, w3, w4, stg, rsl, gm, a, b, qh, kk, vv, kT, vT, oh, ofull, goh, gpo, lse, heads_t,
        x1, xs, xs_out, hact, gpb, segc, segr, facc, gq, gw1, gw2, gw3, gw4, gw5, xl1, xl2, xl3, xl4, xl5,
        zl1, zl2, zl3, zl4, zl5, cl, yl, ps1, ps2, ps3, ps5, pl1, pl2, pl3, pl5, tt, V, vg, snd, rcv,
        credx, credz, aw, uw, dw, x_in, gA, gU, gD, near,
    ) = rest[7:]
    W = {1: w1, 2: w2, 3: w3, 4: w4}
    GW = {1: gw1, 2: gw2, 3: gw3, 4: gw4, 5: gw5}
    XL = {1: xl1, 2: xl2, 3: xl3, 4: xl4, 5: xl5}
    ZL = {1: zl1, 2: zl2, 3: zl3, 4: zl4, 5: zl5}
    PS = {1: ps1, 2: ps2, 3: ps3, 5: ps5}
    PL = {1: pl1, 2: pl2, 3: pl3, 5: pl5}
    S = 4
    T, D = x_in.shape
    R = aw.shape[2]
    CH = R * S
    DP = NZ * 2
    ORDER = (1, NZ - 1) + tuple(range(2, NZ - 1))
    FJ = hb.shape[1]

    d = lax.axis_index("dp")
    s = lax.axis_index("seq")
    z, x = d // 2, d % 2
    y, c = s // 2, s % 2
    xp = 1 - x

    def xor(k):
        return ((y + k // 2) % 2) * 2 + (c + k % 2) % 2

    member = xor

    def dev(dd, ss):
        return {"dp": dd, "seq": ss}

    core_peer, y_peer, x_peer = dev(d, xor(1)), dev(d, xor(2)), dev(z * 2 + xp, s)

    def zdev(dz):
        return dev(((z + dz) % NZ) * 2 + x, s)

    count = [0]

    def sems(n):
        first = count[0]
        count[0] += n
        assert count[0] <= SEMS
        return first

    def rc(src, dst, device, i):
        return pltpu.make_async_remote_copy(
            src_ref=src, dst_ref=dst, send_sem=snd.at[i], recv_sem=rcv.at[i],
            device_id=device, device_id_type=MESH,
        )

    pending = []
    sent_weights = []

    def flush():
        for copy in pending:
            copy.wait_send()
        pending.clear()

    def rows(i):
        return pl.ds(pl.multiple_of(i * T, T), T)

    H = T // 2

    def half(i, h):
        return pl.ds(pl.multiple_of(i * T + h * H, H), H)

    def chunk(i):
        return pl.ds(pl.multiple_of(i * CH, CH), CH)

    local = []

    def move(src, dst):
        copy = pltpu.make_async_copy(src, dst, near.at[len(local)])
        local.append(None)
        copy.start()
        return copy

    def write_out(ends):
        i = len(local)
        local.append(ends)
        pltpu.make_async_copy(*ends(), near.at[i]).start()

    class Gather:
        def __init__(self, view, i):
            self.c1, self.c2, self.c3 = [], [], []
            for h in range(2):
                own, across = view.at[half(s, h)], view.at[half(xor(2), h)]
                self.c1.append(rc(own, own, core_peer, i + h))
                self.c2.append(rc(own, own, y_peer, i + 2 + h))
                self.c3.append(rc(across, across, core_peer, i + 4 + h))

        def start(self, h):
            self.c2[h].start()
            self.c1[h].start()

        def core(self):
            self.c1[0].wait_recv()
            self.c1[1].wait_recv()

        def forward(self, h):
            self.c2[h].wait_recv()
            self.c3[h].start()

        def last(self, h):
            self.c3[h].wait_recv()

        def done(self):
            pending.extend(self.c1 + self.c2 + self.c3)

    ag_sems = {
        (g, l): sems(2 * NZ - 1 if g != 2 else 2 * NZ + DP - 2) for g in W for l in range(2)
    }

    def part(g, dd):
        if g == 2:
            return pl.ds(pl.multiple_of(dd * CH + c * (CH // 2), 16), CH // 2)
        return chunk(dd)

    def ag_z(g, l, *steps):
        i = ag_sems[g, l]
        own = W[g].at[l, part(g, d)]
        for dz in steps or ORDER:
            rc(own, own, zdev(dz), i + dz - 1).start()
            sent_weights.append((g, i + dz - 1))

    def ag_x(g, l, *steps):
        i = ag_sems[g, l]
        for dz in steps:
            ref = W[g].at[l, part(g, ((z - dz + NZ) % NZ) * 2 + x)]
            if dz:
                rc(ref, ref, zdev(dz), i + dz - 1).wait_recv()
            rc(ref, ref, x_peer, i + NZ - 1 + dz).start()
            sent_weights.append((g, i + NZ - 1 + dz))

    def ag_done(g, l):
        i = ag_sems[g, l] + NZ - 1
        for dz in range(NZ):
            ref = W[g].at[l, part(g, dz)]
            rc(ref, ref, x_peer, i + dz).wait_recv()

    def ag_core(g, l, start):
        i = ag_sems[g, l] + 2 * NZ - 2
        for k in range(1, DP):
            ref = W[g].at[l, part(g, (d + k) % DP)]
            copy = rc(ref, ref, core_peer, i + k)
            if start:
                copy.start()
                sent_weights.append((g, i + k))
            else:
                copy.wait_recv()

    red_sems = {g: sems(2 * NZ + 1 + DP if g == 2 else 2 * NZ + S - 2) for g in range(1, 6)}

    def columns(g, l):
        return g == 2 and l == 0

    def own_part(g, l, dd):
        rows_of = part(g, dd)
        return (rows_of, pl.ds(pl.multiple_of(y * (D // 2), 128), D // 2)) if columns(g, l) else (rows_of,)

    def landing(g, l, k):
        return (k, slice(None), slice(0, D // 2)) if columns(g, l) else (k,)

    def x_copy(g, l, dz):
        zi = (z + dz) % NZ
        return rc(
            GW[g].at[own_part(g, l, zi * 2 + xp)], XL[g].at[landing(g, l, dz)], x_peer,
            red_sems[g] + dz,
        )

    def z_copy(g, l, dz):
        return rc(
            GW[g].at[own_part(g, l, ((z + dz) % NZ) * 2 + x)], ZL[g].at[landing(g, l, dz - 1)],
            zdev(dz), red_sems[g] + NZ - 1 + dz,
        )

    def s_copies(g, l):
        i = red_sems[g] + 2 * NZ - 2
        return [
            rc(PS[g].at[(s + ds) % S], PL[g].at[s], dev(d, (s + ds) % S), i + ds)
            for ds in range(1, S)
        ]

    def half_copies(l, action):
        i = red_sems[2] + 2 * NZ - 1
        for k in range(2):
            to = 2 * c + k
            copy = pltpu.make_async_remote_copy(
                src_ref=PS[2].at[landing(2, l, k)], dst_ref=PL[2].at[landing(2, l, y)],
                send_sem=snd.at[i + k],
                recv_sem=rcv.at[i + y], device_id=dev(d, to), device_id_type=MESH,
            )
            pl.when(to != s)(functools.partial(action, copy))

    def half_arrivals(l):
        i = red_sems[2] + 2 * NZ - 1
        for k in range(2):
            ref = PL[2].at[landing(2, l, k)]
            copy = rc(ref, ref, core_peer, i + k)
            pl.when(2 * k + s // 2 != s)(lambda copy=copy: copy.wait_recv())

    def core_copies(l):
        i = red_sems[2] + 2 * NZ + 1
        other = CH // 2 * (1 - c)
        return [
            rc(
                gw2.at[pl.ds(pl.multiple_of(k * CH + other, 16), CH // 2)], cl.at[k], core_peer, i + k
            )
            for k in range(DP)
        ]

    def red_core(l):
        for copy in core_copies(l):
            copy.start()

    def core_sum(l):
        for k, copy in enumerate(core_copies(l)):
            copy.wait_recv()
            gw2[part(2, k)] = (gw2[part(2, k)].astype(F32) + cl[k].astype(F32)).astype(BF16)

    def y_copies():
        theirs = pl.ds(pl.multiple_of((1 - y) * (D // 2), 128), D // 2)
        return [rc(gw2.at[part(2, k), theirs], yl.at[k], y_peer, y_sems + k) for k in range(DP)]

    def red_y():
        core_sum(0)
        for copy in y_copies():
            copy.start()

    def y_sum():
        for k, copy in enumerate(y_copies()):
            copy.wait_recv()
            mine = own_part(2, 0, k)
            gw2[mine] = (gw2[mine].astype(F32) + yl[k].astype(F32)).astype(BF16)

    def red_x(g, l):
        if l == 0 and g != 5:
            pl.semaphore_wait(credx.at[g], 1)
        if g == 2:
            y_sum() if l == 0 else core_sum(l)
        for dz in ORDER + (0,):
            x_copy(g, l, dz).start()

    def red_z(g, l, *steps):
        for dz in steps or ORDER + (0,):
            x_copy(g, l, dz).wait_recv()
            mine = own_part(g, l, ((z + dz) % NZ) * 2 + x)
            GW[g][mine] = (
                GW[g][mine].astype(F32) + XL[g][landing(g, l, dz)].astype(F32)
            ).astype(BF16)
            if dz:
                if l == 0 and g != 5 and dz == ORDER[0]:
                    pl.semaphore_wait(credz.at[g], NZ - 1)
                z_copy(g, l, dz).start()
            elif l == 1 and g != 5:
                pl.semaphore_signal(credx.at[g], 1, device_id=x_peer, device_id_type=MESH)

    def red_sum(g, l):
        total = GW[g][own_part(g, l, d)].astype(F32)
        for dz in ORDER:
            z_copy(g, l, dz).wait_recv()
            total = total + ZL[g][landing(g, l, dz - 1)].astype(F32)
        for dz in ORDER:
            z_copy(g, l, dz).wait_send()
        for dz in range(NZ):
            x_copy(g, l, dz).wait_send()
        if g == 2:
            for copy in core_copies(l) + (y_copies() if l == 0 else []):
                copy.wait_send()
        if l == 1 and g != 5:
            for dz in range(1, NZ):
                pl.semaphore_signal(credz.at[g], 1, device_id=zdev(dz), device_id_type=MESH)
        if g == 4:
            gD[l] = total
            write_out(lambda: (gD.at[l], gD_hbm.at[l]))
            return
        if g == 5:
            tt[0:CH, :] = total
        wide = total.shape[1]
        pad = jnp.zeros((PS[g].shape[1] - R, wide), F32)
        for k in range(2 if g == 2 else S):
            piece = jnp.concatenate([total[R * k : R * (k + 1)], pad], axis=0)
            PS[g][landing(g, l, k)] = piece.astype(BF16)
        if g == 2:
            half_copies(l, lambda copy: copy.start())

            @pl.when(s // 2 == c)
            def _():
                PL[2][landing(2, l, y)] = PS[2][landing(2, l, y)]
            return
        PL[g][s] = PS[g][s]
        for copy in s_copies(g, l):
            copy.start()

    def red_write(g, l):
        if g == 2:
            half_arrivals(l)
            two = [PL[2][landing(2, l, k)].astype(F32)[0:R] for k in range(2)]
            gA[l, 3] = jnp.concatenate(two, axis=1) if l == 0 else two[0] + two[1]
            write_out(lambda: (gA.at[l, 3], gA_hbm.at[l, 3]))
            half_copies(l, lambda copy: copy.wait_send())
            return
        for copy in s_copies(g, l):
            copy.wait_recv()
        parts = [PL[g][k].astype(F32)[0:R] for k in range(S)]
        if g == 1:
            gA[l, 0] = jnp.concatenate([p[:, 0:192] for p in parts], axis=1)
            gA[l, 1] = jnp.concatenate(
                [q for p in parts for q in (p[:, 256:384], p[:, 192:256])], axis=1
            )
            gA[l, 2] = jnp.concatenate([p[:, 384:576] for p in parts], axis=1)
            write_out(lambda: (gA.at[l, 0:3], gA_hbm.at[l, 0:3]))
        elif g == 3:
            gU[l] = jnp.concatenate(
                [parts[k][:, FJ * i : FJ * (i + 1)] for i in range(DP) for k in range(S)], axis=1
            )
            write_out(lambda: (gU.at[l], gU_hbm.at[l]))
        else:
            biases = jnp.transpose(tt[...])
            tt[0:R, :] = parts[0] + parts[1] + parts[2] + parts[3]
            vectors = jnp.transpose(tt[...])
            for k in range(2):
                gV[k] = vectors[16 * k : 16 * k + 8, 0:R]
                gB[k : k + 1, :] = biases[16 * k + 8 : 16 * k + 9, 0:CH]
        for copy in s_copies(g, l):
            copy.wait_send()

    parity = [0]
    scatter_sems = (sems(5), sems(5))
    gather_sems = (sems(6), sems(6), sems(6))
    forward_sems, backward_sems, y_sems = sems(3), sems(6), sems(DP)

    class Scatter:
        def __init__(self, shifted=False):
            base = parity[0] * 3
            i = scatter_sems[parity[0]]
            parity[0] = 1 - parity[0]
            self.base = base
            self.shifted = shifted
            self.y_at = 3 * T if shifted else 2 * T
            self.r1 = rc(stg.at[T : 2 * T], rsl.at[base + 1], core_peer, i)
            self.r0, self.r2 = [], []
            for h in range(2):
                part = pl.ds(h * H, H)
                self.r0.append(rc(stg.at[part], rsl.at[base, part], core_peer, i + 1 + h))
                at = pl.ds(self.y_at + h * H, H)
                self.r2.append(rc(stg.at[at], rsl.at[base + 2, part], y_peer, i + 3 + h))

        def slot(self, k, h=None):
            at = 1 + k - 2 * (k // 3) if self.shifted else k
            return rows(at) if h is None else half(at, h)

        def send_core(self, h=None):
            if h is None:
                stg[T : 2 * T] = facc[self.slot(1)].astype(BF16)
                self.r1.start()
            else:
                stg[h * H : (h + 1) * H] = facc[self.slot(3, h)].astype(BF16)
                self.r0[h].start()

        def send_y(self, h):
            self.r0[h].wait_recv()
            stg[self.y_at + h * H : self.y_at + (h + 1) * H] = (
                facc[self.slot(2, h)] + rsl[self.base, h * H : (h + 1) * H].astype(F32)
            ).astype(BF16)
            self.r2[h].start()

        def core_sent(self):
            for copy in (self.r1, *self.r0):
                copy.wait_send()

        def received(self, h):
            if h == 0:
                self.r1.wait_recv()
            self.r2[h].wait_recv()
            self.r2[h].wait_send()
            own = slice(h * H, (h + 1) * H)
            return rsl[self.base + 1, own].astype(F32) + rsl[self.base + 2, own].astype(F32)

        def finish(self, h):
            return facc[self.slot(0, h)] + self.received(h)

    loads = [
        move(src, dst)
        for src, dst in (
            (aw_hbm, aw), (uw_hbm, uw), (x_hbm.at[0], gm.at[0, rows(s)]), (dw_hbm, dw),
            (x_hbm.at[0], x_in), (cot_hbm.at[0], gm.at[1, rows(s)]),
        )
    ]
    barrier = pltpu.get_barrier_semaphore()
    greeted = [core_peer, y_peer, dev(d, xor(3)), x_peer] + [zdev(dz) for dz in range(1, NZ)]
    for device in greeted:
        pl.semaphore_signal(barrier, inc=1, device_id=device, device_id_type=MESH)

    tt[...] = jnp.zeros_like(tt)
    tt[64:72, 0:R] = lv[0]
    tt[72:80, 0:R] = lv[1]
    tt[80:82, 0:CH] = hb[...]
    turned = jnp.transpose(tt[...])
    lane128 = lax.broadcasted_iota(jnp.int32, (1, 128), 1)
    vec_cols = jnp.where(lane128 < 80, turned[0:R, :], 0.0)[:, 64:128]
    bias_cols = jnp.where((lane128 >= 80) & (lane128 < 82), turned[0:CH, :], 0.0)
    loads[0].wait()
    for k in range(S):
        o = 192 * k
        two = []
        for l in range(2):
            wq, wk, wv = aw[l, 0], aw[l, 1], aw[l, 2]
            tail = vec_cols if l == 0 else jnp.zeros((R, 64), F32)
            two.append(
                jnp.concatenate(
                    [wq[:, o : o + 192], wk[:, o + 128 : o + 192], wk[:, o : o + 128],
                     wv[:, o : o + 192], tail],
                    axis=1,
                )
            )
        stg[144 * k : 144 * k + 48, 0:640] = jnp.concatenate(two, axis=0).astype(BF16)
    loads[1].wait()
    for k in range(S):
        two = [
            jnp.concatenate(
                [uw[l][:, (m * S + k) * FJ : (m * S + k + 1) * FJ] for m in range(DP)], axis=1
            )
            for l in range(2)
        ]
        stg[144 * k + 48 : 144 * k + 96, :] = jnp.concatenate([aw[0, 3], aw[1, 3]], axis=0).astype(BF16)
        stg[144 * k + 96 : 144 * k + 144, :] = jnp.concatenate(two, axis=0).astype(BF16)
    for load in loads[2:]:
        load.wait()
    pl.semaphore_wait(barrier, len(greeted))

    def piece_rows(k):
        return pl.multiple_of(k * 144, 16)

    def send_pieces(source, target):
        i = sems(S - 1)
        copies = []
        for ds in (2, 3, 1):
            to = xor(ds)
            copies.append(rc(source(to), target, dev(d, to), i + ds - 1))
        for copy in copies:
            copy.start()
        return copies

    pieces1 = send_pieces(
        lambda to: stg.at[pl.ds(piece_rows(to), 48), 0:640], rsl.at[s, 0:48, 0:640]
    )
    pieces2 = send_pieces(
        lambda to: stg.at[pl.ds(pl.multiple_of(piece_rows(to) + 48, 16), 96), :], rsl.at[s, 48:144, :]
    )
    gather_x = Gather(gm.at[0], gather_sems[0])
    gather_x.start(0)
    gather_x.start(1)
    w4[0, chunk(d)] = dw[0].astype(BF16)
    ag_z(4, 0, *ORDER[:2])
    ag_x(4, 0, 0)
    w4[1, chunk(d)] = dw[1].astype(BF16)
    ag_x(4, 1, 0)
    rsl[s, 0:48, 0:640] = stg[pl.ds(piece_rows(s), 48), 0:640]
    rsl[s, 48:144, :] = stg[pl.ds(pl.multiple_of(piece_rows(s) + 48, 16), 96), :]
    vg[...] = jnp.zeros_like(vg)
    for copy in pieces1:
        copy.wait_recv()
    got = [rsl[k, 0:48, 0:640].astype(F32) for k in range(S)]
    for l in range(2):
        full = jnp.concatenate([g[R * l : R * (l + 1)] for g in got], axis=0)
        if l == 0:
            full = jnp.concatenate([full[:, 0:512], full[:, 512:640] + bias_cols], axis=1)
        w1[l, chunk(d)] = full.astype(BF16)
    ag_z(1, 0)
    ag_x(1, 0, 0)
    ag_x(4, 0, ORDER[0])

    bounds = []
    running = jnp.int32(0)
    for k in range(SEGS):
        running = running + lens[0, k]
        bounds.append(running)
    N = S * T

    def segments(shape, dim):
        place = lax.broadcasted_iota(jnp.int32, shape, dim)
        seg = jnp.zeros(shape, jnp.int32)
        for bound in bounds:
            seg = seg + jnp.where(place >= bound, 1, 0)
        return jnp.where(seg == SEGS - 1, SEGS + place, seg)

    segr[...] = segments((8, N), 1)
    segc[...] = segments((N, 128), 0)

    ag_x(1, 0, ORDER[0])
    for copy in pieces2:
        copy.wait_recv()
    for g, at in ((2, 48), (3, 96)):
        got = [rsl[k, at : at + 48, :].astype(F32) for k in range(S)]
        for l in range(2):
            W[g][l, chunk(d)] = jnp.concatenate(
                [piece[R * l : R * (l + 1)] for piece in got], axis=0
            ).astype(BF16)
    for copy in pieces1 + pieces2:
        copy.wait_send()
    ag_x(1, 0, ORDER[1])
    ag_x(1, 0, *ORDER[2:])
    ag_z(2, 0)
    ag_z(3, 0)
    ag_z(4, 0, *ORDER[2:])
    ag_x(2, 0, 0)
    ag_x(3, 0, 0)
    gather_x.core()
    gather_x.forward(0)
    gather_x.forward(1)
    gather_cot = Gather(gm.at[1], gather_sems[2])
    gather_cot.start(0)
    gather_cot.start(1)
    ag_done(1, 0)
    V[...] = jnp.transpose(w1[0, :, 512:640].astype(F32))[64:96]
    gather_x.last(0)
    gather_x.last(1)
    gather_x.done()

    def vec(l, k):
        return V[8 * l + k : 8 * l + k + 1, :]

    def own_heads(row):
        total = jnp.zeros((1, 192), F32)
        for k in range(S):
            total = total + jnp.where(s == k, row[:, 192 * k : 192 * (k + 1)], 0.0)
        return total

    def at_heads(part):
        total = jnp.zeros((1, D), F32)
        for k in range(S):
            spread = [jnp.zeros((1, 192), F32)] * S
            spread[k] = part
            total = total + jnp.where(s == k, jnp.concatenate(spread, axis=1), 0.0)
        return total

    low = lax.broadcasted_iota(jnp.int32, (T, 128), 1) < 64
    low_rows = lax.broadcasted_iota(jnp.int32, (128, QBLOCK), 0) < 64

    def project_heads(l):
        bias = jnp.concatenate(
            [own_heads(vec(l, 2)), jnp.zeros((1, 192), F32), own_heads(vec(l, 3)), jnp.zeros((1, 64), F32)],
            axis=1,
        )

        @pl.loop(0, S)
        def _(i):
            r = rows(i)
            if l == 0:
                unit, _ = norm_parts(gm[0, r].astype(F32))
                a[0, r] = (unit * vec(0, 0) + vec(0, 1)).astype(BF16)
            full = (nn(a[l, r], w1[l]) + bias).astype(BF16).astype(F32)
            t0, t1, t2, t3, t4 = (full[:, 128 * j : 128 * (j + 1)] for j in range(5))
            t1r = pltpu.roll(t1, 64, 1)
            v4 = jnp.where(low, t4, 0.0)
            qh[l, 0, r] = (jnp.where(low, t0, 0.0) * SCALE_SCORE).astype(BF16)
            qh[l, 1, r] = (jnp.where(low, 0.0, t0) * SCALE_SCORE).astype(BF16)
            qh[l, 2, r] = (jnp.where(low, t1, 0.0) * SCALE_SCORE).astype(BF16)
            kk[l, 0, r] = t2.astype(BF16)
            kk[l, 1, r] = t1r.astype(BF16)
            vv[l, 0, r] = t3.astype(BF16)
            vv[l, 1, r] = v4.astype(BF16)
            kT[l, 0, :, r] = jnp.transpose(t2).astype(BF16)
            kT[l, 1, :, r] = jnp.transpose(t1r).astype(BF16)
            vT[0, :, r] = jnp.transpose(t3).astype(BF16)
            vT[1, :, r] = jnp.transpose(v4).astype(BF16)

    def by_queries(qb, block):
        q = pl.ds(pl.multiple_of(qb * QBLOCK, QBLOCK), QBLOCK)
        edge = (qb == 0) | (qb == N // QBLOCK - 1)
        for size, here in ((EDGE_KEYS, edge), (KEYS, jnp.logical_not(edge))):
            k = pl.ds(pl.multiple_of((qb // 2) * (N - size), 128), size)
            pl.when(here)(functools.partial(block, q, k))

    def keep_head(h, part):
        p = h // 2
        heads_t[p] = jnp.where(low_rows & (h == 1), heads_t[p], part)

    def attend_block(l, q, k):
        @pl.loop(0, 3)
        def _(h):
            p = h // 2
            allowed = jnp.concatenate([segc[k, :]] * 2, axis=1) == segr[0:1, q]
            scores = jnp.where(allowed, nt(kk[l, p, k], qh[l, h, q]), -1e30)
            top = jnp.max(scores, axis=0, keepdims=True)
            grown = jnp.exp(scores - top)
            total = jnp.sum(grown, axis=0, keepdims=True)
            lse[l, h, :, q] = jnp.broadcast_to(top + jnp.log(total), (8, QBLOCK))
            keep_head(h, nn(vT[p, :, k], grown.astype(BF16)) / total)

        for p in range(2):
            oh[l, q, 128 * p : 128 * (p + 1)] = jnp.transpose(heads_t[p]).astype(BF16)

    def attend(l, points):
        order = (2, 3, 1)
        copies = [
            rc(oh.at[l, rows(xor(k))], goh.at[rows(s)], dev(d, xor(k)), forward_sems + k - 1)
            for k in order
        ]

        @pl.loop(0, N // QBLOCK)
        def _(i):
            for at, action in points.items():
                pl.when(i == at)(action)
            by_queries(
                member((2 + i) * (1 - i // 2) + (3 - i) * (i // 2)), functools.partial(attend_block, l)
            )
            for at in range(3):
                pl.when(i == at)(copies[at].start)

        goh[rows(s)] = oh[l, rows(s)]
        pending.extend(copies)
        return copies

    def attend_grad_block(l, q, k):
        @pl.loop(0, 3)
        def _(h):
            p = h // 2

            def tile(i):
                return pl.ds(pl.multiple_of(128 * i, 128), 128)

            head = jnp.where(low == (h != 1), goh[q, tile(p)].astype(F32), 0.0)
            inner = jnp.sum(
                jnp.transpose(head * oh[l, q, tile(p)].astype(F32)), axis=0, keepdims=True
            )
            head = head.astype(BF16)
            queries = qh[l, h, q]
            allowed = jnp.concatenate([segc[k, :]] * 2, axis=1) == segr[0:1, q]
            scores = jnp.where(allowed, nt(kk[l, p, k], queries), -1e30)
            prob = jnp.exp(scores - lse[l, h, 0:1, q])
            grad = nt(vv[l, p, k], head)
            grad = (prob * (grad - inner)).astype(BF16)
            facc[k, tile(2 + p)] += nn(prob.astype(BF16), head)
            facc[k, tile(p)] += nn(grad, queries)
            keep_head(h, nn(kT[l, p, :, k], grad) * SCALE_SCORE)

        gq[q, 0:128] = jnp.transpose(heads_t[0]).astype(BF16)
        gq[q, 128:256] = jnp.transpose(jnp.where(low_rows, heads_t[1], 0.0)).astype(BF16)

    def attend_grad(l, copies, points):
        facc[:, 0:512] = jnp.zeros((N, 512), F32)

        @pl.loop(0, N // QBLOCK)
        def _(i):
            for at in range(1, S):
                pl.when(i == at)(lambda at=at: (copies[0, at].wait(), copies[1, at].wait())[0])
            for at, action in points.items():
                pl.when(i == at)(action)
            by_queries(member(i), functools.partial(attend_grad_block, l))

        @pl.loop(0, S)
        def _(i):
            r = rows(i)
            other = pltpu.roll(facc[r, 128:256], 64, 1)
            gq[r, 128:256] = (gq[r, 128:256].astype(F32) + other).astype(BF16)
            gq[r, 256:384] = facc[r, 0:128].astype(BF16)
            gq[r, 384:512] = facc[r, 256:384].astype(BF16)
            gq[r, 512:640] = facc[r, 384:512].astype(BF16)

    def exchange(h, copies):
        for ds in (2, 3, 1):
            to = xor(ds)
            copies[h, ds] = rc(
                gq.at[half(to, h), 0:256], goh.at[half(s, h)], dev(d, to),
                backward_sems + 3 * h + ds - 1,
            )
            copies[h, ds].start()

    def up_rows(l, r):
        pre = nn(b[l, r], w3[l]) + V[16 + l : 17 + l, :]
        cdf = 0.5 * (1.0 + lax.erf(pre * 0.7071067811865476))
        density = jnp.exp(-0.5 * pre * pre) * 0.3989422804014327
        hact[l, r] = (pre * cdf).astype(BF16)
        gpb[l, r] = (cdf + pre * density).astype(BF16)

    def up_chip(l, gather, points):
        @pl.loop(0, 2)
        def _(k):
            pl.when(k == 1)(gather.core)
            for at, action in points.items():
                pl.when(k == at)(action)
            up_rows(l, rows(member(k)))

    def up_across(l, gather, h):
        gather.forward(h)

        @pl.loop(0, 2)
        def _(q):
            pl.when(q == 1)(lambda: gather.last(h))
            up_rows(l, half(member(2 + q), h))

    def scatter_rows(term, shifted=False, across=True):
        scatter = Scatter(shifted)

        @pl.loop(0, S)
        def _(i):
            k, h = 3 - i % 2, i // 2
            facc[scatter.slot(k, h)] = term(half(member(k), h))
            pl.when(i == 0)(lambda: scatter.send_core(0))
            pl.when(i == 2)(lambda: scatter.send_core(1))
            if across:
                pl.when(i == 2)(lambda: scatter.send_y(0))

        @pl.loop(0, 2)
        def _(i):
            k = 1 - i
            facc[scatter.slot(k)] = term(rows(member(k)))
            pl.when(i == 0)(scatter.send_core)
            if across:
                pl.when(i == 0)(lambda: scatter.send_y(1))

        return scatter

    def back_rows(l, scatter, r, slot):
        grad_act = nt(gm[l, r], w4[l])
        grad_pre = (grad_act * gpb[l, r].astype(F32)).astype(BF16)
        gpb[l, r] = grad_pre
        facc[slot] = nt(grad_pre, w3[l])
        vg[16 * l + 8 : 16 * l + 9, :] += jnp.sum(grad_pre.astype(F32), axis=0, keepdims=True)

    def back_chip(l, scatter, gather):
        @pl.loop(0, 2)
        def _(i):
            k = i if gather is not None else 1 - i
            if gather is not None:
                pl.when(i == 1)(gather.core)
            back_rows(l, scatter, rows(member(k)), scatter.slot(k))
            pl.when(k == 1)(scatter.send_core)

    def back_across(l, scatter, gather, h):
        if gather is not None:
            gather.forward(h)

        @pl.loop(0, 2)
        def _(i):
            k = 2 + i if gather is not None else 3 - i
            if gather is not None:
                pl.when(i == 1)(lambda: gather.last(h))
            back_rows(l, scatter, half(member(k), h), scatter.slot(k, h))
            pl.when(k == 3)(lambda: scatter.send_core(h))

    def weight_grad(g, left, right):
        @pl.loop(0, 2)
        def _(i):
            m = pl.ds(pl.multiple_of(i * 384, 384), 384)
            GW[g][m, :] = tn(left(m), right()).astype(BF16)

    def column(values):
        return jnp.sum(values.astype(F32), axis=0, keepdims=True)

    last = ORDER[2:]
    for l in range(2):
        project_heads(l)
        if l == 0:
            ag_x(2, 0, *ORDER[:2])

            def core_stage():
                ag_done(2, 0)
                ag_core(2, 0, True)
                ag_x(3, 0, ORDER[1])
                gather_cot.core()
                gather_cot.forward(0)
                gather_cot.forward(1)

            copies = attend(
                0, {1: lambda: ag_x(2, 0, *last), 2: lambda: ag_x(3, 0, ORDER[0]), 3: core_stage}
            )
        else:

            def core_stage():
                ag_done(2, 1)
                ag_core(2, 1, True)

            copies = attend(
                1,
                {
                    1: lambda: ag_x(3, 1, *last),
                    2: lambda: ag_x(4, 1, ORDER[0]),
                    3: core_stage,
                },
            )
            ag_x(4, 1, ORDER[1])
        for copy in copies:
            copy.wait_recv()
        ag_core(2, l, False)
        ofull[l] = jnp.concatenate(
            [goh[T * k : T * (k + 1)].astype(F32)[:, 0:192] for k in range(S)], axis=1
        ).astype(BF16)
        before = x_in[...].astype(F32) if l == 0 else xs[...]
        middle = before + (nn(ofull[l], w2[l]) + vec(l, 4))
        x1[l] = middle
        unit, _ = norm_parts(middle)
        b[l, rows(s)] = (unit * vec(l, 5) + vec(l, 6)).astype(BF16)
        gather_b = Gather(b.at[l], gather_sems[1])
        gather_b.start(0)
        gather_b.start(1)
        if l == 0:
            ag_x(3, 0, *last)
            ag_z(1, 1)
            ag_z(2, 1)
            ag_x(4, 0, ORDER[1])
            ag_x(1, 1, 0)
            gather_cot.last(0)
            gather_cot.last(1)
            gather_cot.done()
        ag_done(3, l)
        if l == 1:
            up_chip(1, gather_b, {1: lambda: ag_x(4, 1, *last)})
            break
        up_chip(0, gather_b, {1: lambda: ag_x(4, 0, *last)})
        ag_x(2, 1, 0)
        ag_x(3, 1, 0)
        ag_z(3, 1)
        ag_z(4, 1)
        up_across(0, gather_b, 0)
        up_across(0, gather_b, 1)
        gather_b.done()
        ag_done(4, 0)
        scatter = scatter_rows(lambda r: nn(hact[0, r], w4[0]))
        ag_x(1, 1, *ORDER)
        scatter.core_sent()
        flush()
        gather_a = Gather(a.at[1], gather_sems[0])
        for h in range(2):
            own = slice(h * H, (h + 1) * H)
            after = x1[0, own] + (scatter.finish(h) + vec(0, 7))
            xs[own] = after
            unit, _ = norm_parts(after)
            a[1, half(s, h)] = (unit * vec(1, 0) + vec(1, 1)).astype(BF16)
            gather_a.start(h)
        ag_x(2, 1, *ORDER)
        ag_x(3, 1, ORDER[0])
        ag_done(1, 1)
        gather_a.core()
        gather_a.forward(0)
        ag_x(3, 1, ORDER[1])
        gather_a.forward(1)
        gather_a.last(0)
        gather_a.last(1)
        gather_a.done()

    for l in (1, 0):
        first = l == 1
        scatter = Scatter()

        def down_grad():
            weight_grad(4, lambda m: hact[l, :, m], lambda: gm[l])
            red_x(4, l)

        if first:
            ag_done(4, 1)
            back_chip(1, scatter, None)
            up_across(1, gather_b, 0)
            back_across(1, scatter, None, 0)
            scatter.send_y(0)
            up_across(1, gather_b, 1)
            gather_b.done()
            down_grad()
            back_across(1, scatter, None, 1)
            scatter.send_y(1)
        else:
            back_chip(0, scatter, gather)
            red_z(1, 1, ORDER[1])
            back_across(0, scatter, gather, 0)
            scatter.send_y(0)
            red_z(1, 1, *last)
            back_across(0, scatter, gather, 1)
            gather.done()
            red_z(1, 1, 0)
            scatter.send_y(1)
            red_z(2, 1, *ORDER[:2])
            down_grad()
            red_z(2, 1, *last, 0)
            red_sum(3, 1)
        vg[16 * l + 7 : 16 * l + 8, :] = column(gm[l, rows(s)])
        weight_grad(3, lambda m: b[l, :, m], lambda: gpb[l])
        red_x(3, l)
        scatter.core_sent()
        if first:
            scatter_out = scatter_rows(lambda r: nn(hact[1, r], w4[1]), True, False)
        else:
            out_copy.wait()
        flush()
        copies = {}
        sums = [0.0, 0.0, 0.0]
        for h in range(2):
            own = slice(h * H, (h + 1) * H)
            if h and not first:
                red_z(4, 0, ORDER[0])
            grad_b = scatter.finish(h)
            grad_x1, gain, shift = norm_back(x1[l, own], grad_b, vec(l, 5))
            grad_x1 = grad_x1 + (gm[1, half(s, h)].astype(F32) if first else xs[own])
            if first:
                xs_out[own] = x1[1, own] + facc[scatter_out.slot(0, h)]
            x1[l, own] = grad_x1
            gpo[own] = grad_x1.astype(BF16)
            back = nt(gpo[own], w2[l])
            for k in range(S):
                gq[half(k, h), 0:256] = jnp.concatenate(
                    [back[:, 192 * k : 192 * (k + 1)], jnp.zeros((H, 64), F32)], axis=1
                ).astype(BF16)
            exchange(h, copies)
            goh[half(s, h)] = gq[half(s, h), 0:256]
            sums = [sums[0] + gain, sums[1] + shift, sums[2] + column(gpo[own])]
        vg[16 * l + 5 : 16 * l + 6, :] = sums[0]
        vg[16 * l + 6 : 16 * l + 7, :] = sums[1]
        vg[16 * l + 4 : 16 * l + 5, :] = sums[2]
        if first:
            scatter_out.send_y(0)
            scatter_out.send_y(1)
        if first:
            red_z(4, 1, ORDER[0])
            points = {
                1: lambda: red_z(4, 1, ORDER[1]),
                3: lambda: red_z(4, 1, *last),
            }
        else:

            def late():
                red_z(4, 0, *last)
                red_sum(2, 1)
                weight_grad(2, lambda m: ofull[0, :, m], lambda: gpo[...])
                red_core(0)

            points = {
                0: lambda: red_sum(1, 1),
                1: lambda: red_z(4, 0, ORDER[1]),
                2: late,
                3: lambda: (red_y(), red_write(3, 1), red_write(1, 1))[1],
            }
        attend_grad(l, copies, points)
        sums = column(gq[...])
        vg[16 * l + 2 : 16 * l + 3, :] = at_heads(sums[:, 0:192])
        vg[16 * l + 3 : 16 * l + 4, :] = at_heads(sums[:, 384:576])
        if first:
            scatter_out.core_sent()
        red_z(4, l, 0)
        if not first:
            red_z(3, 0, ORDER[0])
        scatter = scatter_rows(lambda r: nt(gq[r], w1[l]))
        red_z(3, l, ORDER[0] if first else ORDER[1])
        weight_grad(1, lambda m: a[l, :, m], lambda: gq[...])
        red_x(1, l)
        if first:
            weight_grad(2, lambda m: ofull[1, :, m], lambda: gpo[...])
            red_core(1)
            red_z(3, 1, ORDER[1])
        if not first:
            red_z(3, 0, *last)
        if first:
            red_x(2, 1)
            for h in range(2):
                own = slice(h * H, (h + 1) * H)
                gpo[own] = (xs_out[own] + (scatter_out.received(h) + vec(1, 7))).astype(BF16)
            out_copy = move(gpo, out.at[0])
            red_z(3, 1, *last)
            red_sum(4, 1)
        else:
            red_x(2, 0)
            red_write(2, 1)
            red_z(3, 0, 0)
        scatter.core_sent()
        flush()
        sums = [0.0, 0.0]
        if first:
            gather = Gather(gm.at[0], gather_sems[0])
        for h in range(2):
            own = slice(h * H, (h + 1) * H)
            grad_a = scatter.finish(h)
            before = xs[own] if first else x_in[own].astype(F32)
            grad, gain, shift = norm_back(before, grad_a, vec(l, 0))
            grad = grad + x1[l, own]
            sums = [sums[0] + gain, sums[1] + shift]
            if first:
                xs[own] = grad
                gm[0, half(s, h)] = grad.astype(BF16)
                gather.start(h)
            else:
                gpo[own] = grad.astype(BF16)
        vg[16 * l : 16 * l + 1, :] = sums[0]
        vg[16 * l + 1 : 16 * l + 2, :] = sums[1]
        if not first:
            write_out(lambda: (gpo, gin.at[0]))
            gw5[...] = jnp.transpose(vg[...]).astype(BF16)
            red_x(5, 0)
        if first:
            red_z(3, 1, 0)
            red_z(1, 1, ORDER[0])

    red_z(1, 0, ORDER[0])
    red_sum(4, 0)
    red_z(1, 0, *ORDER[1:], 0)
    red_z(2, 0)
    red_z(5, 0)
    red_sum(3, 0)
    red_sum(1, 0)
    red_write(3, 0)
    red_sum(2, 0)
    red_sum(5, 0)
    red_write(1, 0)
    red_write(2, 0)
    red_write(5, 0)
    for i, ends in enumerate(local):
        if ends is not None:
            pltpu.make_async_copy(*ends(), near.at[i]).wait()
    flush()
    for g, i in sent_weights:
        ref = W[g].at[0, part(g, 0)]
        rc(ref, ref, x_peer, i).wait_send()


def fused_step(inputs, cotangent, image_lengths, attention, upward, downward, vectors, bias_up):
    DP = lax.axis_size("dp")
    S = lax.axis_size("seq")
    NZ = DP // 2
    L = attention.shape[0]
    T, D = inputs.shape[1], inputs.shape[2]
    N = S * T
    R = attention.shape[2]
    CH = R * S
    RP = (R + 15) // 16 * 16
    FJ = bias_up.shape[1]
    vmem, hbm = pl.BlockSpec(memory_space=pltpu.VMEM), pl.BlockSpec(memory_space=pl.ANY)
    V = pltpu.VMEM
    widths = {1: 640, 2: D, 3: D, 4: D, 5: 128}
    scratch = [
        V((L, D, 640), BF16), V((L, D, D), BF16), V((L, D, D), BF16), V((L, D, D), BF16),
        V((4 * T, D), BF16),
        V((6, T, D), BF16),
        V((L, N, D), BF16), V((L, N, D), BF16), V((L, N, D), BF16),
        V((L, 3, N, 128), BF16), V((L, 2, N, 128), BF16), V((L, 2, N, 128), BF16),
        V((L, 2, 128, N), BF16), V((2, 128, N), BF16),
        V((L, N, 256), BF16), V((L, T, D), BF16),
        V((N, 256), BF16), V((T, D), BF16),
        V((L, 3, 8, N), F32), V((2, 128, QBLOCK), F32),
        V((L, T, D), F32), V((T, D), F32), V((T, D), F32),
        V((L, N, D), BF16), V((L, N, D), BF16),
        V((N, 128), jnp.int32), V((8, N), jnp.int32),
        V((N, D), F32),
        V((N, 640), BF16),
        *[V((D, widths[g]), BF16) for g in range(1, 6)],
        *[V((NZ, CH // 2 if g == 2 else CH, widths[g]), BF16) for g in range(1, 6)],
        *[V((NZ - 1, CH // 2 if g == 2 else CH, widths[g]), BF16) for g in range(1, 6)],
        V((DP, CH // 2, D), BF16), V((DP, CH // 2, D // 2), BF16),
        *[V((2 if g == 2 else S, RP, widths[g]), BF16) for g in (1, 2, 3, 5)],
        *[V((2 if g == 2 else S, RP, widths[g]), BF16) for g in (1, 2, 3, 5)],
        V((128, 128), F32), V((32, D), F32), V((128, D), F32),
        pltpu.SemaphoreType.DMA((SEMS,)), pltpu.SemaphoreType.DMA((SEMS,)),
        pltpu.SemaphoreType.REGULAR((8,)), pltpu.SemaphoreType.REGULAR((8,)),
        V(attention.shape, F32), V(upward.shape, F32), V(downward.shape, F32),
        V((T, D), BF16),
        V(attention.shape, F32), V(upward.shape, F32), V(downward.shape, F32),
        pltpu.SemaphoreType.DMA((16,)),
    ]
    return pl.pallas_call(
        functools.partial(step_kernel, NZ),
        out_shape=(
            jax.ShapeDtypeStruct(inputs.shape, BF16),
            jax.ShapeDtypeStruct(inputs.shape, BF16),
            jax.ShapeDtypeStruct(attention.shape, F32),
            jax.ShapeDtypeStruct(upward.shape, F32),
            jax.ShapeDtypeStruct(downward.shape, F32),
            jax.ShapeDtypeStruct(vectors.shape, F32),
            jax.ShapeDtypeStruct(bias_up.shape, F32),
        ),
        in_specs=[hbm, hbm, pl.BlockSpec(memory_space=pltpu.SMEM), hbm, hbm, hbm, vmem, vmem],
        out_specs=(hbm,) * 5 + (vmem,) * 2,
        scratch_shapes=scratch,
        compiler_params=pltpu.CompilerParams(
            collective_id=0, has_side_effects=True, vmem_limit_bytes=VMEM_BYTES
        ),
    )(inputs, cotangent, image_lengths, attention, upward, downward, vectors, bias_up)


def fits_fused(inputs, attention, upward, bias_up, dp_count, seq_count):
    own_rows, width = attention.shape[2], attention.shape[3]
    return (
        seq_count == 4
        and dp_count == 8
        and inputs.shape == (1, QBLOCK, 768)
        and width == 768
        and own_rows % 8 == 0
        and upward.shape[2] == seq_count * width
        and bias_up.shape[1] % 16 == 0
    )


def update_kernel(rate, *refs):
    for member in range(5):
        gradient, master, moment, average = (refs[5 * k + member][...] for k in range(4))
        results = optimizer_step(gradient, master, moment, average, rate)
        for k in range(5):
            refs[22 + 5 * member + k][...] = results[k]
    for k in range(2):
        refs[47 + k][...] = refs[20 + k][...]


def fused_update(rate, output, input_grad, reduced, masters, moments, averages):
    attention, upward, downward, vectors, bias_up = masters
    blocks = [
        pl.BlockSpec((1,) + attention.shape[1:], lambda l: (l, 0, 0, 0)),
        pl.BlockSpec((1,) + upward.shape[1:], lambda l: (l, 0, 0)),
        pl.BlockSpec((1,) + downward.shape[1:], lambda l: (l, 0, 0)),
        pl.BlockSpec((1,) + vectors.shape[1:], lambda l: (l, 0, 0)),
        pl.BlockSpec(bias_up.shape, lambda l: (0, 0)),
    ]
    tokens = pl.BlockSpec((1, output.shape[1] // 2, output.shape[2]), lambda l: (0, l, 0))
    outs, specs = [], []
    for member in range(5):
        for k in range(5):
            outs.append(jax.ShapeDtypeStruct(masters[member].shape, BF16 if k == 4 else F32))
            specs.append(blocks[member])
    outs += [jax.ShapeDtypeStruct(output.shape, BF16)] * 2
    results = pl.pallas_call(
        functools.partial(update_kernel, rate),
        grid=(2,),
        out_shape=outs,
        in_specs=blocks * 4 + [tokens] * 2,
        out_specs=specs + [tokens] * 2,
        compiler_params=pltpu.CompilerParams(vmem_limit_bytes=VMEM_BYTES),
    )(*reduced, *masters, *moments, *averages, output, input_grad)
    return tuple(results[25:]) + tuple(results[:25])


def per_device(
    inputs,
    cotangent,
    image_lengths,
    attention_weight,
    attention_moment,
    attention_average,
    up_weight,
    up_moment,
    up_average,
    down_weight,
    down_moment,
    down_average,
    layer_vectors,
    vector_moment,
    vector_average,
    hidden_bias,
    bias_moment,
    bias_average,
):
    masters = (attention_weight, up_weight, down_weight, layer_vectors, hidden_bias)
    dp_count = lax.axis_size("dp")
    seq_count = lax.axis_size("seq")
    if fits_fused(inputs, attention_weight, up_weight, hidden_bias, dp_count, seq_count):
        output, input_grad, *reduced = fused_step(inputs, cotangent, image_lengths, *masters)
        moments = (attention_moment, up_moment, down_moment, vector_moment, bias_moment)
        averages = (attention_average, up_average, down_average, vector_average, bias_average)
        rate = LEARN_BASE / math.sqrt(inputs.shape[0] * inputs.shape[1] * dp_count * seq_count)
        return fused_update(rate, output, input_grad, reduced, masters, moments, averages)
    else:
        output, input_grad, *reduced = plain_step(inputs, cotangent, image_lengths, masters)
    total_tokens = inputs.shape[0] * inputs.shape[1] * dp_count * seq_count
    step_rate = LEARN_BASE / math.sqrt(total_tokens)
    states = (
        (attention_weight, attention_moment, attention_average),
        (up_weight, up_moment, up_average),
        (down_weight, down_moment, down_average),
        (layer_vectors, vector_moment, vector_average),
        (hidden_bias, bias_moment, bias_average),
    )
    outcome = [output, input_grad]
    for member in range(5):
        master, moment, average = states[member]
        outcome.extend(optimizer_step(reduced[member], master, moment, average, step_rate))
    return tuple(outcome)


def solution(mesh):
    placed = (
        P("dp", "seq", None),
        P("dp", "seq", None),
        P("dp", None),
        P(None, None, ("dp", "seq"), None),
        P(None, None, ("dp", "seq"), None),
        P(None, None, ("dp", "seq"), None),
        P(None, ("dp", "seq"), None),
        P(None, ("dp", "seq"), None),
        P(None, ("dp", "seq"), None),
        P(None, ("dp", "seq"), None),
        P(None, ("dp", "seq"), None),
        P(None, ("dp", "seq"), None),
        P(None, None, ("dp", "seq")),
        P(None, None, ("dp", "seq")),
        P(None, None, ("dp", "seq")),
        P(None, ("dp", "seq")),
        P(None, ("dp", "seq")),
        P(None, ("dp", "seq")),
    )
    return jax.shard_map(
        per_device,
        mesh=mesh,
        in_specs=placed,
        out_specs=(
            P("dp", "seq", None),
            P("dp", "seq", None),
            P(None, None, ("dp", "seq"), None),
            P(None, None, ("dp", "seq"), None),
            P(None, None, ("dp", "seq"), None),
            P(None, None, ("dp", "seq"), None),
            P(None, None, ("dp", "seq"), None),
            P(None, ("dp", "seq"), None),
            P(None, ("dp", "seq"), None),
            P(None, ("dp", "seq"), None),
            P(None, ("dp", "seq"), None),
            P(None, ("dp", "seq"), None),
            P(None, ("dp", "seq"), None),
            P(None, ("dp", "seq"), None),
            P(None, ("dp", "seq"), None),
            P(None, ("dp", "seq"), None),
            P(None, ("dp", "seq"), None),
            P(None, None, ("dp", "seq")),
            P(None, None, ("dp", "seq")),
            P(None, None, ("dp", "seq")),
            P(None, None, ("dp", "seq")),
            P(None, None, ("dp", "seq")),
            P(None, ("dp", "seq")),
            P(None, ("dp", "seq")),
            P(None, ("dp", "seq")),
            P(None, ("dp", "seq")),
            P(None, ("dp", "seq")),
        ),
        check_vma=False,
    )
```

profile of v0, /device:TPU:0, one launch (start us, length us, event | category | flops | bytes accessed | tf_op | source)
XLA Modules:
  0.0 223.8 jit_solution(5270289973313795253)
XLA Ops:
  0.7 216.7 %shard_map.385 = (bf16[1,256,768]{2,1,0:T(8,128)(2,1)}, bf16[1,256,768]{2,1,0:T(8,128)(2,1)}, f32[2,4,24,768]{3,2,1,0:T(8,128)}, f32[2,24,3072]{2,1,0:T(8,128)},...) custom-call(bf16[1,256,768]{2,1,0:T(8,128)(2,1)} %x_hbm.1, bf16[1,256,768]{2,1,0:T(8,128)(2,1)} %cot_hbm.1, ...), custom_call_target="tpu_custom_call" | custom-call | tf_op jit(solution)/shard_map/pallas_call | solution.py:1440
  217.4 6.2 %shard_map.386 = (f32[2,4,24,768]{3,2,1,0:T(8,128)}, f32[2,4,24,768]{3,2,1,0:T(8,128)}, f32[2,4,24,768]{3,2,1,0:T(8,128)}, f32[2,4,24,768]{3,2,1,0:T(8,128)}, bf...) custom-call(f32[2,4,24,768]{3,2,1,0:T(8,128)} %get-tuple-element.61., ...), custom_call_target="tpu_custom_call" | custom-call | tf_op jit(solution)/shard_map/pallas_call | solution.py:1499
where the time goes:
time: 224 us
  Pallas kernels  223 us (100%)
    pallas_call x1, Pallas kernels, fused_step(): pl.pallas_call(functools.partial(step_kernel, NZ), out_shape=(jax.ShapeDt...  217 us
    pallas_call x1, Pallas kernels, fused_update(): pl.pallas_call(functools.partial(update_kernel, rate), grid=(2,), out_sha...  6.24 us

commit v1 on v0

--- a/solution.py
+++ b/solution.py
@@ -373,13 +373,13 @@
     )
 
 
-SEMS = 178
+SEMS = 108
 
 
 def step_kernel(NZ, x_hbm, cot_hbm, lens, aw_hbm, uw_hbm, dw_hbm, lv, hb, *rest):
     (out, gin, gA_hbm, gU_hbm, gD_hbm, gV, gB) = rest[:7]
     (
-        w1, w2, w3, w4, stg, rsl, gm, a, b, qh, kk, vv, kT, vT, oh, ofull, goh, gpo, lse, heads_t,
+        w1, w2, w3, w4, stg, rsl, gm, a, b, qh, kk, vv, kT, vT, oh, ofull, goh, gpo, lse, heads_t, wsnd, wrcv,
         x1, xs, xs_out, hact, gpb, segc, segr, facc, gq, gw1, gw2, gw3, gw4, gw5, xl1, xl2, xl3, xl4, xl5,
         zl1, zl2, zl3, zl4, zl5, cl, yl, ps1, ps2, ps3, ps5, pl1, pl2, pl3, pl5, tt, V, vg, snd, rcv,
         credx, credz, aw, uw, dw, x_in, gA, gU, gD, near,
@@ -431,8 +431,13 @@
             device_id=device, device_id_type=MESH,
         )
 
+    def weight_copy(ref, device, g, l, i):
+        return pltpu.make_async_remote_copy(
+            src_ref=ref, dst_ref=ref, send_sem=wsnd.at[2 * (g - 1) + l], recv_sem=wrcv.at[i],
+            device_id=device, device_id_type=MESH,
+        )
+
     pending = []
-    sent_weights = []
 
     def flush():
         for copy in pending:
@@ -490,9 +495,11 @@
         def done(self):
             pending.extend(self.c1 + self.c2 + self.c3)
 
-    ag_sems = {
-        (g, l): sems(2 * NZ - 1 if g != 2 else 2 * NZ + DP - 2) for g in W for l in range(2)
-    }
+    ag_sems, taken = {}, 0
+    for g in W:
+        for l in range(2):
+            ag_sems[g, l] = taken
+            taken += 2 * NZ - 1 if g != 2 else 2 * NZ + DP - 2
 
     def part(g, dd):
         if g == 2:
@@ -503,32 +510,29 @@
         i = ag_sems[g, l]
         own = W[g].at[l, part(g, d)]
         for dz in steps or ORDER:
-            rc(own, own, zdev(dz), i + dz - 1).start()
-            sent_weights.append((g, i + dz - 1))
+            weight_copy(own, zdev(dz), g, l, i + dz - 1).start()
 
     def ag_x(g, l, *steps):
         i = ag_sems[g, l]
         for dz in steps:
             ref = W[g].at[l, part(g, ((z - dz + NZ) % NZ) * 2 + x)]
             if dz:
-                rc(ref, ref, zdev(dz), i + dz - 1).wait_recv()
-            rc(ref, ref, x_peer, i + NZ - 1 + dz).start()
-            sent_weights.append((g, i + NZ - 1 + dz))
+                weight_copy(ref, zdev(dz), g, l, i + dz - 1).wait_recv()
+            weight_copy(ref, x_peer, g, l, i + NZ - 1 + dz).start()
 
     def ag_done(g, l):
         i = ag_sems[g, l] + NZ - 1
         for dz in range(NZ):
             ref = W[g].at[l, part(g, dz)]
-            rc(ref, ref, x_peer, i + dz).wait_recv()
+            weight_copy(ref, x_peer, g, l, i + dz).wait_recv()
 
     def ag_core(g, l, start):
         i = ag_sems[g, l] + 2 * NZ - 2
         for k in range(1, DP):
             ref = W[g].at[l, part(g, (d + k) % DP)]
-            copy = rc(ref, ref, core_peer, i + k)
+            copy = weight_copy(ref, core_peer, g, l, i + k)
             if start:
                 copy.start()
-                sent_weights.append((g, i + k))
             else:
                 copy.wait_recv()
 
@@ -1389,9 +1393,9 @@
         if ends is not None:
             pltpu.make_async_copy(*ends(), near.at[i]).wait()
     flush()
-    for g, i in sent_weights:
-        ref = W[g].at[0, part(g, 0)]
-        rc(ref, ref, x_peer, i).wait_send()
+    for g in W:
+        for l in range(2):
+            weight_copy(W[g].at[l, 0 : (2 * NZ - 1) * CH], x_peer, g, l, 0).wait_send()
 
 
 def fused_step(inputs, cotangent, image_lengths, attention, upward, downward, vectors, bias_up):
@@ -1418,6 +1422,7 @@
         V((L, N, 256), BF16), V((L, T, D), BF16),
         V((N, 256), BF16), V((T, D), BF16),
         V((L, 3, 8, N), F32), V((2, 128, QBLOCK), F32),
+        pltpu.SemaphoreType.DMA((8,)), pltpu.SemaphoreType.DMA((70,)),
         V((L, T, D), F32), V((T, D), F32), V((T, D), F32),
         V((L, N, D), BF16), V((L, N, D), BF16),
         V((N, 128), jnp.int32), V((8, N), jnp.int32),

time: 224 us -> 223 us (level)
  no operation moved by 1% of the time
where the time goes in v1:
time: 223 us
  Pallas kernels  222 us (100%)
    pallas_call x1, Pallas kernels, fused_step(): pl.pallas_call(functools.partial(step_kernel, NZ), out_shape=(jax.ShapeDt...  216 us
    pallas_call x1, Pallas kernels, fused_update(): pl.pallas_call(functools.partial(update_kernel, rate), grid=(2,), out_sha...  6.24 us

profile of v1, /device:TPU:0, one launch (start us, length us, event | category | flops | bytes accessed | tf_op | source)
XLA Modules:
  0.0 223.2 jit_solution(16443264387131089725)
XLA Ops:
  0.7 216.1 %shard_map.385 = (bf16[1,256,768]{2,1,0:T(8,128)(2,1)}, bf16[1,256,768]{2,1,0:T(8,128)(2,1)}, f32[2,4,24,768]{3,2,1,0:T(8,128)}, f32[2,24,3072]{2,1,0:T(8,128)},...) custom-call(bf16[1,256,768]{2,1,0:T(8,128)(2,1)} %x_hbm.1, bf16[1,256,768]{2,1,0:T(8,128)(2,1)} %cot_hbm.1, ...), custom_call_target="tpu_custom_call" | custom-call | tf_op jit(solution)/shard_map/pallas_call | solution.py:1445
  216.8 6.2 %shard_map.386 = (f32[2,4,24,768]{3,2,1,0:T(8,128)}, f32[2,4,24,768]{3,2,1,0:T(8,128)}, f32[2,4,24,768]{3,2,1,0:T(8,128)}, f32[2,4,24,768]{3,2,1,0:T(8,128)}, bf...) custom-call(f32[2,4,24,768]{3,2,1,0:T(8,128)} %get-tuple-element.61., ...), custom_call_target="tpu_custom_call" | custom-call | tf_op jit(solution)/shard_map/pallas_call | solution.py:1504
